TPU v7x, 32 devices: a whole 2x2x4 slice. The times are simulated.
32 devices in a mesh: section: 8 (over z, y), expert: 2 (over core), shard: 2 (over x).
Axes of the slice: x: 2, y: 2, z: 4, core: 2. Of those that a mesh axis runs over, the one named last changes fastest.
Arguments:
- routes: int32 [8, 4, 64, 2], P('section', None, 'expert'), may hold values from 0 to 7, as said below
- route_probs: float32 [8, 4, 64, 2], P('section', None, 'expert'), may hold values from 0.2 to 1
- example_ids: int32 [4, 2, 32], P(None, 'expert'), may hold values from 0 to 1, never falling along the last dimension, each value on 1 to 24 neighbouring positions
- top_cotangent: bfloat16 [4, 64, 6144], P(None, 'expert', 'shard'), may hold values from -6 to 6
- branch_cotangent: bfloat16 [8, 4, 64, 6144], P('section', None, 'expert', 'shard'), may hold values from -4 to 4
- hidden_acts: bfloat16 [8, 2, 4, 32, 16384], P('section', 'expert', None, None, 'shard'), may hold values from -6 to 6
- basis_hidden: bfloat16 [8, 2, 16384, 256], P('section', 'expert', 'shard'), may hold values from -0.046875 to 0.046875
- basis_model: bfloat16 [8, 2, 6144, 1024], P('section', 'expert', 'shard'), may hold values from -0.078125 to 0.078125
Outputs:
- eigen_correction: float32 [8, 2, 256, 1024], P('section', 'expert', None, 'shard')
Inputs may be any that keep to these rules, and one draw needn't show every extreme that they name: `routes`: each token names 2 different experts of the 8. Within the 32 tokens of one owner in one micro-batch no expert is named more than 16 times, and exactly one expert is named 16 times. In one micro-batch of every layer that expert is the same for every owner and is below 2. `example_ids`: Non-decreasing along each owner's 32 tokens of a micro-batch; each example has 1 to 24 tokens.
All inputs are finite; a program needn't handle non-finite values.
Results may differ from a plain program's by a relative error of at most 0.0047.
Values may be sent and summed in bfloat16 or wider, within the bound.
A program may use at most 128 MiB of HBM per device.

v0:
```python
import jax
import jax.numpy as jnp
from jax import lax
from jax.sharding import PartitionSpec as P

SEQS = 2


def carried_in(shard, axis, join, neutral):
    count = lax.axis_size(axis)
    place = lax.axis_index(axis)
    ahead = count - 1 - place
    gathered = lax.all_gather(shard.astype(jnp.bfloat16), axis)
    state = jnp.zeros_like(shard) + jnp.asarray(neutral, shard.dtype)

    def one(step, state):
        source = count - 1 - step
        return join(state, lax.dynamic_index_in_dim(gathered, source, 0, False).astype(shard.dtype))

    return lax.fori_loop(0, ahead, one, state)


def add_terms(earlier_term, later_term):
    return earlier_term + later_term


def dispatch_tables(route_rows, prob_rows, example_rows, experts, capacity):
    expert_hit = (route_rows[:, :, :, None] == jnp.arange(experts, dtype=jnp.int32)).astype(
        jnp.int32
    )
    expert_count = jnp.sum(expert_hit, axis=2)
    slot_rank = jnp.cumsum(expert_count, axis=1) - expert_count
    expert_prob = jnp.sum(expert_hit.astype(jnp.float32) * prob_rows[:, :, :, None], axis=2)
    slot_match = (slot_rank[:, :, :, None] == jnp.arange(capacity, dtype=jnp.int32)) & (
        expert_count[:, :, :, None] > 0
    )
    dispatch_weight = jnp.where(slot_match, expert_prob[:, :, :, None], jnp.float32(0.0))
    slot_example = jnp.sum(jnp.where(slot_match, example_rows[:, :, None, None] + 1, 0), axis=1) - 1
    return (dispatch_weight, slot_example)


def example_squares(rotated_hidden, rotated_model, slot_example, examples):
    member = slot_example[:, None, :] == jnp.arange(examples, dtype=jnp.int32)[None, :, None]
    masked = jnp.where(
        member[:, :, :, None], rotated_hidden[:, None, :, :], jnp.zeros((), jnp.bfloat16)
    )
    example_grad = jnp.einsum(
        "osci,ocj->osij", masked, rotated_model, preferred_element_type=jnp.float32
    )
    return jnp.sum(example_grad * example_grad, axis=(0, 1))


def on_device(
    routes,
    route_probs,
    example_ids,
    top_cotangent,
    branch_cotangent,
    hidden_acts,
    basis_hidden,
    basis_model,
):
    experts = lax.axis_size("expert")
    shards = lax.axis_size("shard")
    batches = top_cotangent.shape[0]
    capacity = hidden_acts.shape[3] // experts
    local_cols = basis_model.shape[3] // shards
    branch_wide = branch_cotangent[0].astype(jnp.float32)
    later_sum = carried_in(branch_wide, "section", add_terms, jnp.zeros_like(branch_wide))
    cotangent = top_cotangent.astype(jnp.float32) + later_sum
    dispatch_weight, slot_example = dispatch_tables(
        routes[0], route_probs[0], example_ids[:, 0], experts, capacity
    )
    send_rows = jnp.einsum(
        "ntec,ntd->necd", dispatch_weight, cotangent, precision=lax.Precision.HIGHEST
    ).astype(jnp.bfloat16)
    hidden_basis = basis_hidden[0, 0]
    model_basis = basis_model[0, 0]
    got_rows = lax.all_to_all(send_rows, "expert", split_axis=1, concat_axis=1, tiled=True)
    got_examples = lax.all_to_all(slot_example, "expert", split_axis=1, concat_axis=1, tiled=True)
    slot_total = experts * capacity
    hidden_rows = hidden_acts[0, 0, 0 : 0 + batches]
    hidden_part = jnp.einsum(
        "nsf,fk->nsk", hidden_rows, hidden_basis, preferred_element_type=jnp.float32
    )
    rotated_hidden = lax.psum(hidden_part, "shard").astype(jnp.bfloat16)
    flat_rows = got_rows.reshape(batches * slot_total, got_rows.shape[3])
    model_sum = lax.psum_scatter(
        lax.dot_general(
            model_basis, flat_rows, (((0,), (1,)), ((), ())), preferred_element_type=jnp.float32
        ),
        "shard",
        scatter_dimension=0,
        tiled=True,
    )
    rotated_model = model_sum.T.astype(jnp.bfloat16)
    rotated_model = rotated_model.reshape(batches, experts, capacity, local_cols)
    rotated_hidden = rotated_hidden.reshape(batches, experts, capacity, rotated_hidden.shape[2])
    square_sum = jnp.zeros((rotated_hidden.shape[3], local_cols), jnp.float32)
    for micro_batch in range(batches):
        square_sum = square_sum + example_squares(
            rotated_hidden[micro_batch], rotated_model[micro_batch], got_examples[micro_batch], SEQS
        )
    example_count = batches * experts * SEQS
    return (square_sum / example_count)[None, None]


def solution(mesh):
    return jax.shard_map(
        on_device,
        mesh=mesh,
        in_specs=(
            P("section", None, "expert", None),
            P("section", None, "expert", None),
            P(None, "expert", None),
            P(None, "expert", "shard"),
            P("section", None, "expert", "shard"),
            P("section", "expert", None, None, "shard"),
            P("section", "expert", "shard", None),
            P("section", "expert", "shard", None),
        ),
        out_specs=P("section", "expert", None, "shard"),
        check_vma=False,
    )
```

profile of v0, /device:TPU:0, one launch (start us, length us, event | category | flops | bytes accessed | tf_op | source)
XLA Modules:
  0.0 170.2 jit_solution(7071166291822774587)
XLA Ops:
  6.5 0.7 all-gather.2.cloned.1.call-update
  7.3 0.7 copy.41
  8.0 0.1 copy.42
  8.2 0.1 copy.44
  8.3 0.7 broadcast_add_fusion
  9.0 0.2 select_reduce_fusion
  9.2 0.6 copy_add_fusion
  9.8 3.2 %all-to-all-start = ((s32[4,2,16]{2,0,1:T(4,128)}), s32[4,2,16]{2,0,1:T(4,128)S(1)}, u32[]{:S(2)}, u32[]{:S(2)}) async-start(s32[4,2,16]{2,0,1:T(4,128)} %copy_add_fusion), calls=%async_computation | async-start | bytes 8192 | tf_op jit(solution)/shard_map/all_to_all | solution.py:80
  13.1 0.7 copy.47
  13.8 0.6 all-to-all-done
  14.4 2.9 %fusion.2 = f32[4,32,256]{2,1,0:T(8,128)S(1)} fusion(bf16[1,1,8192,256]{3,2,1,0:T(8,128)(2,1)} %param.16, bf16[1,1,4,32,8192]{4,3,2,1,0:T(8,128)(2,1)S(1)} %copy-done), kind=kOutput, calls=%fused_computation.3 | convolution fusion | flops 536870912 | bytes 6422528 | tf_op jit(solution)/shard_map/nsf,fk->nsk/dot_general | solution.py:83
  17.3 94.0 %all-gather.2.cloned.1.call-done = bf16[8,4,32,3072]{3,2,1,0:T(8,128)(2,1)} async-done(((bf16[1,4,32,3072]{3,2,1,0:T(8,128)(2,1)}), bf16[8,4,32,3072]{3,2,1,0:T(8,128)(2,1)}) %all-gather.2.cloned.1.call-update) | async-done | bytes 6291472 | tf_op jit(solution)/shard_map/all_gather | solution.py:13
  111.3 1.3 broadcast_in_dim.110
  112.6 20.5 %while.12 = (s32[]{:T(128)}, f32[4,32,3072]{2,1,0:T(8,128)}, s32[]{:T(128)}, bf16[8,4,32,3072]{3,2,1,0:T(8,128)(2,1)}, s32[]{:T(128)}, /*index=5*/s32[]{:T(128)}, s32[]{:T(128)}, s32[]{:T(128)}) while((s32[]{:T(128)}, f32[4,32,3072]{2,1,0:T(8,128)}, s32[]{:T(128)}, bf16[8,4,32,3072]{3,2,1,0:T(8,128)(2,1)}, s32[]{:T(128)}, ...), condition=%wide.region_6.7_spmd, body=%wide.region_5.6_spmd.sunk | while | flops 786438 | bytes 3932303 | solution.py:20
  112.6 3.0 %convert_add_fusion.2 = f32[4,32,3072]{2,1,0:T(8,128)} fusion(f32[4,32,3072]{2,1,0:T(8,128)} %get-tuple-element.117, bf16[8,4,32,3072]{3,2,1,0:T(8,128)(2,1)} %get-tuple-element.127, s32[]{:T(128)S(6)} %select_n.46), kind=kLoop, calls=%fused_computation.clone.1 | loop fusion | flops 786432 | bytes 3932164 | tf_op jit(solution)/shard_map/while/body/add | solution.py:24
  115.6 2.9 %convert_add_fusion.2 = f32[4,32,3072]{2,1,0:T(8,128)} fusion(f32[4,32,3072]{2,1,0:T(8,128)} %get-tuple-element.117, bf16[8,4,32,3072]{3,2,1,0:T(8,128)(2,1)} %get-tuple-element.127, s32[]{:T(128)S(6)} %select_n.46), kind=kLoop, calls=%fused_computation.clone.1 | loop fusion | flops 786432 | bytes 3932164 | tf_op jit(solution)/shard_map/while/body/add | solution.py:24
  118.5 2.9 %convert_add_fusion.2 = f32[4,32,3072]{2,1,0:T(8,128)} fusion(f32[4,32,3072]{2,1,0:T(8,128)} %get-tuple-element.117, bf16[8,4,32,3072]{3,2,1,0:T(8,128)(2,1)} %get-tuple-element.127, s32[]{:T(128)S(6)} %select_n.46), kind=kLoop, calls=%fused_computation.clone.1 | loop fusion | flops 786432 | bytes 3932164 | tf_op jit(solution)/shard_map/while/body/add | solution.py:24
  121.4 2.9 %convert_add_fusion.2 = f32[4,32,3072]{2,1,0:T(8,128)} fusion(f32[4,32,3072]{2,1,0:T(8,128)} %get-tuple-element.117, bf16[8,4,32,3072]{3,2,1,0:T(8,128)(2,1)} %get-tuple-element.127, s32[]{:T(128)S(6)} %select_n.46), kind=kLoop, calls=%fused_computation.clone.1 | loop fusion | flops 786432 | bytes 3932164 | tf_op jit(solution)/shard_map/while/body/add | solution.py:24
  124.3 2.9 %convert_add_fusion.2 = f32[4,32,3072]{2,1,0:T(8,128)} fusion(f32[4,32,3072]{2,1,0:T(8,128)} %get-tuple-element.117, bf16[8,4,32,3072]{3,2,1,0:T(8,128)(2,1)} %get-tuple-element.127, s32[]{:T(128)S(6)} %select_n.46), kind=kLoop, calls=%fused_computation.clone.1 | loop fusion | flops 786432 | bytes 3932164 | tf_op jit(solution)/shard_map/while/body/add | solution.py:24
  127.3 2.9 %convert_add_fusion.2 = f32[4,32,3072]{2,1,0:T(8,128)} fusion(f32[4,32,3072]{2,1,0:T(8,128)} %get-tuple-element.117, bf16[8,4,32,3072]{3,2,1,0:T(8,128)(2,1)} %get-tuple-element.127, s32[]{:T(128)S(6)} %select_n.46), kind=kLoop, calls=%fused_computation.clone.1 | loop fusion | flops 786432 | bytes 3932164 | tf_op jit(solution)/shard_map/while/body/add | solution.py:24
  130.2 2.9 %convert_add_fusion.2 = f32[4,32,3072]{2,1,0:T(8,128)} fusion(f32[4,32,3072]{2,1,0:T(8,128)} %get-tuple-element.117, bf16[8,4,32,3072]{3,2,1,0:T(8,128)(2,1)} %get-tuple-element.127, s32[]{:T(128)S(6)} %select_n.46), kind=kLoop, calls=%fused_computation.clone.1 | loop fusion | flops 786432 | bytes 3932164 | tf_op jit(solution)/shard_map/while/body/add | solution.py:24
  133.1 2.8 %convolution_convert_fusion = bf16[4,2,16,3072]{3,2,1,0:T(8,128)(2,1)S(1)} fusion(f32[4,32,3072]{2,1,0:T(8,128)} %get-tuple-element.61, bf16[4,32,3072]{2,1,0:T(8,128)(2,1)S(1)} %copy-done.1, f32[4,32,2]{1,2,0:T(2,128)S(1)} %copy.48, s32[4,32,2]{1,2,0:T(2,128)S(1)} %copy.44, pred[4,32,2]{1,2,0:T(4,128)(4,1)S(1)} %copy.45), kind=kOutput, calls=%fused_computation.5 | convolution fusion | flops 152186880 | bytes 3148032 | tf_op jit(solution)/shard_map/ntec,ntd->necd/dot_general | solution.py:74
  136.0 4.4 %all_to_all.10 = bf16[4,2,16,3072]{3,2,0,1:T(8,128)(2,1)S(1)} all-to-all(bf16[4,2,16,3072]{3,2,0,1:T(8,128)(2,1)S(1)} %copy.49), channel_id=1, replica_groups=mesh['section'=8,'expert'=2,'shard'=2] {'expert'}, dimensions={1} | all-to-all | bytes 1572864 | tf_op jit(solution)/shard_map/all_to_all | solution.py:79
  140.4 4.6 %fusion.8 = f32[1024,128]{0,1:T(8,128)} fusion(bf16[128,3072]{1,0:T(8,128)(2,1)S(1)} %bitcast.66, bf16[1,1,3072,1024]{3,2,1,0:T(8,128)(2,1)} %param.17), kind=kOutput, calls=%fused_computation.14 | convolution fusion | flops 805306368 | bytes 7602176 | tf_op jit(solution)/shard_map/dot_general | solution.py:89
  145.1 12.9 %all-reduce.1 = bf16[4,32,256]{2,1,0:T(8,128)(2,1)S(1)} all-reduce(f32[4,32,256]{2,1,0:T(8,128)S(1)} %fusion.2), channel_id=1, replica_groups=mesh['section'=8,'expert'=2,'shard'=2] {'shard'}, use_global_device_ids=true, to_apply=%region_3.4 | all-reduce | flops 32768 | bytes 196608 | tf_op jit(solution)/shard_map/psum | solution.py:86
  158.1 0.8 reduce-scatter.2.cloned.1.call-done
  158.9 1.0 convert_bitcast_fusion
  159.9 0.6 multiply_reduce_fusion
  160.5 0.6 multiply_reduce_fusion.1
  161.1 0.6 multiply_reduce_fusion.3
  161.7 0.6 multiply_reduce_fusion.2
  162.4 1.0 multiply_bitcast_fusion
  (23 shorter events, 0.4 us)
Async XLA Ops:
  6.5 7.8 %copy-start = (bf16[1,1,4,32,8192]{4,3,2,1,0:T(8,128)(2,1)S(1)}, bf16[1,1,4,32,8192]{4,3,2,1,0:T(8,128)(2,1)}, u32[]{:S(2)}) copy-start(bf16[1,1,4,32,8192]{4,3,2,1,0:T(8,128)(2,1)} %param.15) | copy-start | bytes 6291460
  6.5 104.8 %all-gather.2.cloned.1.call-start = ((), (), s32[]{:S(2)}) async-start(), calls=%async_computation.3 | async-start | bytes 7077888 | tf_op jit(solution)/shard_map/all_gather | solution.py:13
  9.8 4.6 %all-to-all-start = ((s32[4,2,16]{2,0,1:T(4,128)}), s32[4,2,16]{2,0,1:T(4,128)S(1)}, u32[]{:S(2)}, u32[]{:S(2)}) async-start(s32[4,2,16]{2,0,1:T(4,128)} %copy_add_fusion), calls=%async_computation | async-start | bytes 8192 | tf_op jit(solution)/shard_map/all_to_all | solution.py:80
  13.0 145.9 %reduce-scatter.2.cloned.1.call-start = ((), (), s32[]{:S(2)}) async-start(), calls=%async_computation.4 | async-start | bytes 786432 | tf_op jit(solution)/shard_map/reduce_scatter | solution.py:88
  112.6 20.5 %copy-start.1 = (bf16[4,32,3072]{2,1,0:T(8,128)(2,1)S(1)}, bf16[4,32,3072]{2,1,0:T(8,128)(2,1)}, u32[]{:S(2)}) copy-start(bf16[4,32,3072]{2,1,0:T(8,128)(2,1)} %param.13) | copy-start | bytes 2359300
Sparse Core Ops, SparseCore 0:
  9.5 101.7 all-gather.1
  145.2 13.6 reduce-scatter.1
where the time goes:
time: 171 us; the launch traced here: 170 us
  waiting for transfers between devices  96.1 us (56%)
  other arithmetic  24.1 us (14%)
  blocking collectives  17.3 us (10%)
  between operations  13.5 us (8%)
  matrix products  12.8 us (7%)
  starting transfers between devices  3.26 us (2%)
  local copies, waits for them, and re-layouts  3.05 us (2%)
    all_gather x1, waiting for transfers between devices, carried_in(): gathered = lax.all_gather(shard.astype(jnp.bfloat16), axis)  94 us
    add x7, other arithmetic, add_terms(): return earlier_term + later_term  20.5 us
    psum x1, blocking collectives, on_device(): rotated_hidden = lax.psum(hidden_part, 'shard').astype(jnp.bfloat16)  12.9 us
    dot_general x1, matrix products, on_device(): lax.dot_general(model_basis, flat_rows, (((0,), (1,)), ((), ())), preferr...  4.64 us
    all_to_all x1, blocking collectives, on_device(): lax.all_to_all(send_rows, 'expert', split_axis=1, concat_axis=1, tiled=True)  4.37 us
  transfers between devices with their start and end apart: 3, of which 3 were waited for; matrix products, arithmetic and copies ran while one was open for 4% of the time, Pallas kernels for 0%

commit v1 on v0

v1 whole, which is shorter than its diff:
```python
import functools

import jax
import jax.numpy as jnp
from jax import lax
from jax.experimental import pallas as pl
from jax.experimental.pallas import tpu as pltpu
from jax.sharding import PartitionSpec as P

SEQS = 2
MESH = pl.DeviceIdType.MESH


def kernel(
    sections,
    routes,
    probs,
    examples,
    top,
    branch,
    hidden,
    basis_hidden,
    basis_model,
    out,
    top_v,
    own_v,
    hidden_v,
    bh_v,
    bm_v,
    pair_in,
    chain_in,
    chain_out,
    swap_out,
    swap_in,
    select_v,
    prob_v,
    ex_out,
    ex_all,
    rows_out,
    rows_all,
    part_out,
    part_own,
    part_in,
    hid_own,
    hid_in,
    hid_sum,
    local_sem,
    pair_s,
    pair_r,
    chain_s,
    chain_r,
    swap_s,
    swap_r,
    rows_s,
    rows_r,
    part_s,
    part_r,
    one_s,
    one_r,
):
    batches, tokens, width = top.shape
    half = width // 2
    cap = rows_out.shape[2]
    section = lax.axis_index("section")
    core = lax.axis_index("expert")
    shard = lax.axis_index("shard")
    low = lax.rem(section, 2)
    high = section // 2
    last = sections // 2 - 1
    partner = {"section": section + 1 - 2 * low}
    other_core = {"expert": 1 - core}
    other_shard = {"shard": 1 - shard}
    cols = part_out.shape[2]
    pieces = bh_v.shape[0]
    depth = bh_v.shape[1]

    def columns(index):
        return pl.ds(pl.multiple_of(index * half, 128), half)

    loads = [
        pltpu.make_async_copy(branch.at[0, :, :, columns(low)], own_v, local_sem.at[0]),
        pltpu.make_async_copy(top.at[:, :, columns(0)], top_v.at[0], local_sem.at[1]),
        pltpu.make_async_copy(top.at[:, :, columns(1)], top_v.at[1], local_sem.at[2]),
        pltpu.make_async_copy(hidden.at[0, 0], hidden_v, local_sem.at[3]),
        pltpu.make_async_copy(
            basis_model.at[0, 0, :, pl.ds(0, cols)], bm_v.at[0], local_sem.at[4]
        ),
        pltpu.make_async_copy(
            basis_model.at[0, 0, :, pl.ds(cols, cols)], bm_v.at[1], local_sem.at[5]
        ),
    ]
    hidden_loads = [
        pltpu.make_async_copy(
            basis_hidden.at[0, 0, pl.ds(p * depth, depth)], bh_v.at[p], local_sem.at[6 + p]
        )
        for p in range(pieces)
    ]
    loads[0].start()
    loads[3].start()
    for load in hidden_loads:
        load.start()
    for index in (1, 2, 4, 5):
        loads[index].start()

    barrier = pltpu.get_barrier_semaphore()
    for target in (partner, other_core, other_shard):
        pl.semaphore_signal(barrier, inc=1, device_id=target, device_id_type=MESH)

    @pl.when(high > 0)
    def _():
        pl.semaphore_signal(
            barrier, inc=1, device_id={"section": section - 2}, device_id_type=MESH
        )

    @pl.when(high < last)
    def _():
        pl.semaphore_signal(
            barrier, inc=1, device_id={"section": section + 2}, device_id_type=MESH
        )

    pl.semaphore_wait(
        barrier, 3 + jnp.where(high > 0, 1, 0) + jnp.where(high < last, 1, 0)
    )

    def remote(source, target, send, receive, device):
        return pltpu.make_async_remote_copy(
            src_ref=source,
            dst_ref=target,
            send_sem=send,
            recv_sem=receive,
            device_id=device,
            device_id_type=MESH,
        )

    def pair_copy(m):
        return remote(
            branch.at[0, m, :, columns(1 - low)],
            pair_in.at[m],
            pair_s.at[m],
            pair_r.at[m],
            partner,
        )

    def chain_copy(m):
        return remote(
            chain_out.at[m], chain_in.at[m], chain_s.at[m], chain_r.at[m],
            {"section": section - 2},
        )

    def swap_copy(m):
        return remote(swap_out.at[m], swap_in.at[m], swap_s.at[m], swap_r.at[m], partner)

    def rows_copy(m):
        return remote(
            rows_out.at[m], rows_all.at[m, core], rows_s.at[m], rows_r.at[m], other_core
        )

    def part_copy(m):
        return remote(part_out.at[m], part_in.at[m], part_s.at[m], part_r.at[m], other_shard)

    ex_copy = remote(ex_out, ex_all.at[core], one_s.at[0], one_r.at[0], other_core)
    hid_copy = remote(hid_own, hid_in, one_s.at[1], one_r.at[1], other_shard)

    for m in range(batches):
        pair_copy(m).start()

    lane_token = lax.broadcasted_iota(jnp.int32, (tokens, tokens), 1)
    row_token = lax.broadcasted_iota(jnp.int32, (tokens, tokens), 0)
    slot_row = lax.broadcasted_iota(jnp.int32, (cap, tokens), 0).astype(jnp.float32)
    for m in range(batches):
        named = routes[0, m]
        weight = probs[0, m]
        example_row = examples[m].astype(jnp.float32)
        for place in range(2):
            expert = core if place == 0 else 1 - core
            hit = named == expert
            count = jnp.sum(jnp.where(hit, 1.0, 0.0), axis=1, keepdims=True)
            prob = jnp.sum(jnp.where(hit, weight, 0.0), axis=1, keepdims=True)
            rank_row = jnp.sum(
                jnp.where(row_token < lane_token, count, 0.0), axis=0, keepdims=True
            )
            count_row = jnp.sum(
                jnp.where(row_token == lane_token, count, 0.0), axis=0, keepdims=True
            )
            prob_row = jnp.sum(
                jnp.where(row_token == lane_token, prob, 0.0), axis=0, keepdims=True
            )
            match = jnp.where(slot_row == rank_row, 1.0, 0.0) * count_row
            slot_prob = jnp.sum(match * prob_row, axis=1, keepdims=True)
            slot_example = jnp.sum(match * (example_row + 1.0), axis=1, keepdims=True) - 1.0
            select_v[m, place * cap : (place + 1) * cap, :] = match.astype(jnp.bfloat16)
            prob_v[m, place * cap : (place + 1) * cap, :] = jnp.broadcast_to(
                slot_prob, (cap, prob_v.shape[2])
            )
            wide = jnp.broadcast_to(slot_example.astype(jnp.int32), (cap, ex_out.shape[2]))
            if place == 0:
                ex_all[core, m] = wide
            else:
                ex_out[m] = wide
    ex_copy.start()

    @pl.when(high == last)
    def _():
        chain_in[...] = jnp.zeros_like(chain_in)

    loads[0].wait()

    def carry(m):
        pair_copy(m).wait_recv()

        @pl.when(high < last)
        def _():
            chain_copy(m).wait_recv()

        own = own_v[m].astype(jnp.float32)
        before = chain_in[m].astype(jnp.float32)

        @pl.when(high > 0)
        def _():
            total = before + own + pair_in[m].astype(jnp.float32)
            chain_out[m] = total.astype(jnp.bfloat16)
            chain_copy(m).start()

        swap_out[m] = (before + jnp.where(low == 1, own, 0.0)).astype(jnp.bfloat16)
        swap_copy(m).start()

    def rotate_hidden():
        loads[3].wait()
        for p in range(pieces):
            hidden_loads[p].wait()
        hid_own[...] = jnp.zeros_like(hid_own)

        def piece(p, _):
            acts = hidden_v[:, :, pl.ds(pl.multiple_of(p * depth, 128), depth)]
            hid_own[...] += jnp.dot(
                acts.reshape(batches * acts.shape[1], depth),
                bh_v[p],
                preferred_element_type=jnp.float32,
            )
            return 0

        lax.fori_loop(0, pieces, piece, 0)
        hid_copy.start()

    def dispatch(m):
        swap_copy(m).wait_recv()
        select = select_v[m]
        pair_select = jnp.where(low == 0, select.astype(jnp.float32), 0.0).astype(jnp.bfloat16)
        slot_prob = prob_v[m][:, :1]

        def pick(matrix, rows):
            return jnp.dot(matrix, rows, preferred_element_type=jnp.float32)

        mine = pick(select, top_v[low, m]) + pick(select, chain_in[m])
        mine = (mine + pick(pair_select, pair_in[m])) * slot_prob
        rest = (pick(select, top_v[1 - low, m]) + pick(select, swap_in[m])) * slot_prob
        mine = mine.astype(jnp.bfloat16)
        rest = rest.astype(jnp.bfloat16)
        rows_out[m, low] = mine[cap:]
        rows_out[m, 1 - low] = rest[cap:]
        rows_copy(m).start()
        rows_all[m, core, low] = mine[:cap]
        rows_all[m, core, 1 - low] = rest[:cap]

    def rotate_model(m):
        rows_copy(m).wait_recv()

        def rotated(block):
            total = None
            for h in range(2):
                rows = jnp.concatenate([rows_all[m, 0, h], rows_all[m, 1, h]], axis=0)
                term = jnp.dot(
                    rows,
                    bm_v[block, h * half : (h + 1) * half, :],
                    preferred_element_type=jnp.float32,
                )
                total = term if total is None else total + term
            return total

        part_out[m] = rotated(1 - shard)
        part_copy(m).start()
        part_own[m] = rotated(shard)

    def squares(m):
        part_copy(m).wait_recv()
        model = (part_own[m] + part_in[m]).astype(jnp.bfloat16)
        hid = hid_sum[m]
        total = None
        for owner in range(2):
            block = hid[owner * cap : (owner + 1) * cap]
            ids = ex_all[owner, m][:, :1]
            for q in range(SEQS):
                masked = jnp.where(ids == q, block, 0.0).astype(jnp.bfloat16)
                grad = lax.dot_general(
                    masked,
                    model[owner * cap : (owner + 1) * cap],
                    (((0,), (0,)), ((), ())),
                    preferred_element_type=jnp.float32,
                )
                total = grad * grad if total is None else total + grad * grad
        out[0, 0] += total

    def step(k, _):
        @pl.when(k < batches)
        def _():
            carry(k)

        @pl.when(k == 0)
        def _():
            rotate_hidden()

        @pl.when(k == 1)
        def _():
            loads[1].wait()
            loads[2].wait()

        @pl.when(jnp.logical_and(k >= 1, k < batches + 1))
        def _():
            dispatch(k - 1)

        @pl.when(k == 2)
        def _():
            loads[4].wait()
            loads[5].wait()

        @pl.when(jnp.logical_and(k >= 2, k < batches + 2))
        def _():
            rotate_model(k - 2)

        @pl.when(k == 3)
        def _():
            ex_copy.wait_recv()
            hid_copy.wait_recv()
            hid = hid_own[...] + hid_in[...]
            hid_sum[...] = hid.reshape(hid_sum.shape)
            out[...] = jnp.zeros_like(out)

        @pl.when(k >= 3)
        def _():
            squares(k - 3)

        return 0

    lax.fori_loop(0, batches + 3, step, 0)
    out[...] = out[...] / (batches * 2 * SEQS)

    for m in range(batches):
        pair_copy(m).wait_send()
        swap_copy(m).wait_send()
        rows_copy(m).wait_send()
        part_copy(m).wait_send()
    ex_copy.wait_send()
    hid_copy.wait_send()

    @pl.when(high > 0)
    def _():
        for m in range(batches):
            chain_copy(m).wait_send()


def on_device(
    routes,
    route_probs,
    example_ids,
    top_cotangent,
    branch_cotangent,
    hidden_acts,
    basis_hidden,
    basis_model,
):
    sections = lax.axis_size("section")
    shards = lax.axis_size("shard")
    batches, tokens, width = top_cotangent.shape
    slots, depth = hidden_acts.shape[3:]
    cap = slots // lax.axis_size("expert")
    rank_hidden = basis_hidden.shape[3]
    cols = basis_model.shape[3] // shards
    half = width // 2
    pieces = 4
    bf16, f32 = jnp.bfloat16, jnp.float32
    vmem = pl.BlockSpec(memory_space=pltpu.VMEM)
    hbm = pl.BlockSpec(memory_space=pl.ANY)
    dma = pltpu.SemaphoreType.DMA
    chunk = (batches, tokens, half)
    flops = 2 * batches * slots * (depth * rank_hidden + width * cols * shards)
    return pl.pallas_call(
        functools.partial(kernel, sections),
        out_shape=jax.ShapeDtypeStruct((1, 1, rank_hidden, cols), f32),
        in_specs=[vmem] * 3 + [hbm] * 5,
        out_specs=vmem,
        scratch_shapes=[
            pltpu.VMEM((2,) + chunk, bf16),
            pltpu.VMEM(chunk, bf16),
            pltpu.VMEM((batches, slots, depth), bf16),
            pltpu.VMEM((pieces, depth // pieces, rank_hidden), bf16),
            pltpu.VMEM((2, width, cols), bf16),
            pltpu.VMEM(chunk, bf16),
            pltpu.VMEM(chunk, bf16),
            pltpu.VMEM(chunk, bf16),
            pltpu.VMEM(chunk, bf16),
            pltpu.VMEM(chunk, bf16),
            pltpu.VMEM((batches, 2 * cap, tokens), bf16),
            pltpu.VMEM((batches, 2 * cap, 128), f32),
            pltpu.VMEM((batches, cap, 128), jnp.int32),
            pltpu.VMEM((2, batches, cap, 128), jnp.int32),
            pltpu.VMEM((batches, 2, cap, half), bf16),
            pltpu.VMEM((batches, 2, 2, cap, half), bf16),
            pltpu.VMEM((batches, slots, cols), f32),
            pltpu.VMEM((batches, slots, cols), f32),
            pltpu.VMEM((batches, slots, cols), f32),
            pltpu.VMEM((batches * slots, rank_hidden), f32),
            pltpu.VMEM((batches * slots, rank_hidden), f32),
            pltpu.VMEM((batches, slots, rank_hidden), f32),
            dma((6 + pieces,)),
            dma((batches,)),
            dma((batches,)),
            dma((batches,)),
            dma((batches,)),
            dma((batches,)),
            dma((batches,)),
            dma((batches,)),
            dma((batches,)),
            dma((batches,)),
            dma((batches,)),
            dma((2,)),
            dma((2,)),
        ],
        compiler_params=pltpu.CompilerParams(
            collective_id=0, has_side_effects=True, vmem_limit_bytes=48 * 1024 * 1024
        ),
        cost_estimate=pl.CostEstimate(
            flops=flops, bytes_accessed=16 * 1024 * 1024, transcendentals=0
        ),
    )(
        routes,
        route_probs,
        example_ids,
        top_cotangent,
        branch_cotangent,
        hidden_acts,
        basis_hidden,
        basis_model,
    )


def solution(mesh):
    return jax.shard_map(
        on_device,
        mesh=mesh,
        in_specs=(
            P("section", None, "expert", None),
            P("section", None, "expert", None),
            P(None, "expert", None),
            P(None, "expert", "shard"),
            P("section", None, "expert", "shard"),
            P("section", "expert", None, None, "shard"),
            P("section", "expert", "shard", None),
            P("section", "expert", "shard", None),
        ),
        out_specs=P("section", "expert", None, "shard"),
        check_vma=False,
    )
```

time: 171 us -> 51.3 us (0.30)
  waiting for transfers between devices: 96.1 us -> 0 us
  Pallas kernels: 0 us -> 44.1 us
  other arithmetic: 24.1 us -> 0 us
  blocking collectives: 17.3 us -> 0 us
  between operations: 13.5 us -> 0.02 us
  matrix products: 12.8 us -> 0 us
  local copies, waits for them, and re-layouts: 3.05 us -> 6.9 us
  starting transfers between devices: 3.26 us -> 0 us
    all_gather x1 -> x0, waiting for transfers between devices: 94 us -> none  [carried_in(): gathered = lax.all_gather(shard.astype(jnp.bfloat16), axis)]
    pallas_call x0 -> x1, Pallas kernels: none -> 44.1 us  [on_device(): pl.pallas_call(functools.partial(kernel, sections), out_shape=jax.ShapeDt...]
    add x8 -> x0, other arithmetic: 21.1 us -> none  [the longest x7 20.5 us: add_terms(): return earlier_term + later_term]
    psum x1 -> x0, blocking collectives: 12.9 us -> none  [on_device(): rotated_hidden = lax.psum(hidden_part, 'shard').astype(jnp.bfloat16)]
    dot_general x7 -> x0, matrix products: 12.8 us -> none  [the longest x1 4.64 us: on_device(): lax.dot_general(model_basis, flat_rows, (((0,), (1,)), ((), ())), preferr...]
    unnamed x4 -> x11, local copies, waits for them, and re-layouts: 0.01 us -> 6.9 us
    all_to_all x1 -> x0, blocking collectives: 4.37 us -> none  [on_device(): lax.all_to_all(send_rows, 'expert', split_axis=1, concat_axis=1, tiled=True)]
    all_to_all x1 -> x0, starting transfers between devices: 3.22 us -> none  [on_device(): lax.all_to_all(slot_example, 'expert', split_axis=1, concat_axis=1, tiled...]
  transfers between devices with their start and end apart: 3 -> 0, of which waited for: 3 -> 0; matrix products, arithmetic and copies ran while one was open for 4% -> 0% of each run, Pallas kernels for 0% -> 0%
where the time goes in v1:
time: 51.3 us; the launch traced here: 51 us
  Pallas kernels  44.1 us (86%)
  local copies, waits for them, and re-layouts  6.9 us (13%)
    pallas_call x1, Pallas kernels, on_device(): pl.pallas_call(functools.partial(kernel, sections), out_shape=jax.ShapeDt...  44.1 us
    unnamed x11, local copies, waits for them, and re-layouts  6.9 us

profile of v1, /device:TPU:0, one launch (start us, length us, event | category | flops | bytes accessed | tf_op | source)
XLA Modules:
  0.0 51.0 jit_solution(16993364740180124361)
XLA Ops:
  0.0 0.8 %copy.9.routes = s32[1,4,32,2]{3,2,1,0:T(8,128)S(1)} copy(s32[1,4,32,2]{2,3,1,0:T(2,128)} %param.8) | data formatting | bytes 2048 | tf_op args[0]
  0.8 0.8 %copy.10.probs = f32[1,4,32,2]{3,2,1,0:T(8,128)S(1)} copy(f32[1,4,32,2]{2,3,1,0:T(2,128)} %param.9) | data formatting | bytes 2048 | tf_op args[1]
  1.6 0.0 copy-start
  1.6 1.6 %copy-done = bf16[1,1,4,32,8192]{4,3,2,1,0:T(8,128)(2,1)S(1)} copy-done((bf16[1,1,4,32,8192]{4,3,2,1,0:T(8,128)(2,1)S(1)}, bf16[1,1,4,32,8192]{4,3,2,1,0:T(8,128)(2,1)}, u32[]{:S(2)}) %copy-start) | copy-done | bytes 2097176
  3.2 0.0 copy-start.1
  3.2 1.1 %copy-done.1 = bf16[4,32,3072]{2,1,0:T(8,128)(2,1)S(1)} copy-done((bf16[4,32,3072]{2,1,0:T(8,128)(2,1)S(1)}, bf16[4,32,3072]{2,1,0:T(8,128)(2,1)}, u32[]{:S(2)}) %copy-start.1) | copy-done | bytes 786456
  4.3 0.0 copy-start.2
  4.3 1.1 %copy-done.2 = bf16[1,4,32,3072]{3,2,1,0:T(8,128)(2,1)S(1)} copy-done((bf16[1,4,32,3072]{3,2,1,0:T(8,128)(2,1)S(1)}, bf16[1,4,32,3072]{3,2,1,0:T(8,128)(2,1)}, u32[]{:S(2)}) %copy-start.2) | copy-done | bytes 786456
  5.4 0.0 copy-start.3
  5.4 0.7 %copy-done.3 = s32[4,1,32]{2,1,0:T(1,128)S(1)} copy-done((s32[4,1,32]{2,1,0:T(1,128)S(1)}, s32[4,1,32]{2,1,0:T(1,128)}, u32[]{:S(2)}) %copy-start.3) | copy-done | bytes 536
  6.1 44.1 %shard_map.82 = f32[1,1,256,512]{3,2,1,0:T(8,128)S(1)} custom-call(s32[1,4,32,2]{3,2,1,0:T(8,128)S(1)} %copy.9.routes, f32[1,4,32,2]{3,2,1,0:T(8,128)S(1)} %copy.10.probs, s32[4,1,32]{2,1,0:T(1,128)S(1)} %copy-done.3, bf16[4,32,3072]{2,1,0:T(8,128)(2,1)S(1)} %copy-done.1, bf16[1,4,32,3072]{3,2,1,0:T(8,128)(2,1)S(1)} %copy-done.2, ...), custom_call_target="tpu_custom_call" | custom-call | flops 1342177280 | bytes 16777216 | tf_op jit(solution)/shard_map/pallas_call | solution.py:386
  50.2 0.8 %copy.12 = f32[1,1,256,512]{3,2,1,0:T(8,128)} copy(f32[1,1,256,512]{3,2,1,0:T(8,128)S(1)} %shard_map.82) | data formatting | bytes 1048576
Async XLA Ops:
  1.6 1.6 %copy-start = (bf16[1,1,4,32,8192]{4,3,2,1,0:T(8,128)(2,1)S(1)}, bf16[1,1,4,32,8192]{4,3,2,1,0:T(8,128)(2,1)}, u32[]{:S(2)}) copy-start(bf16[1,1,4,32,8192]{4,3,2,1,0:T(8,128)(2,1)} %hidden.1) | copy-start | bytes 6291460
  3.2 1.1 %copy-start.1 = (bf16[4,32,3072]{2,1,0:T(8,128)(2,1)S(1)}, bf16[4,32,3072]{2,1,0:T(8,128)(2,1)}, u32[]{:S(2)}) copy-start(bf16[4,32,3072]{2,1,0:T(8,128)(2,1)} %top.1) | copy-start | bytes 2359300
  4.3 1.1 %copy-start.2 = (bf16[1,4,32,3072]{3,2,1,0:T(8,128)(2,1)S(1)}, bf16[1,4,32,3072]{3,2,1,0:T(8,128)(2,1)}, u32[]{:S(2)}) copy-start(bf16[1,4,32,3072]{3,2,1,0:T(8,128)(2,1)} %branch.1) | copy-start | bytes 2359300
  5.4 0.7 %copy-start.3 = (s32[4,1,32]{2,1,0:T(1,128)S(1)}, s32[4,1,32]{2,1,0:T(1,128)}, u32[]{:S(2)}) copy-start(s32[4,1,32]{2,1,0:T(1,128)} %examples.1) | copy-start | bytes 1540

commit v2 on v1

v2 whole, which is shorter than its diff:
```python
import functools

import jax
import jax.numpy as jnp
from jax import lax
from jax.experimental import pallas as pl
from jax.experimental.pallas import tpu as pltpu
from jax.sharding import PartitionSpec as P

SEQS = 2
CHUNK = 256
IN_FLIGHT = 3
MESH = pl.DeviceIdType.MESH


def kernel(
    sections,
    routes,
    probs,
    examples,
    top,
    branch,
    hidden,
    basis_hidden,
    basis_model,
    out,
    routes_v,
    probs_v,
    examples_v,
    top_v,
    own_v,
    hidden_v,
    bh_v,
    bm_v,
    pair_in,
    chain_in,
    chain_out,
    swap_out,
    swap_in,
    select_v,
    prob_v,
    ex_out,
    ex_all,
    rows_out,
    rows_all,
    model_sum,
    part_out,
    part_in,
    hid_own,
    hid_in,
    hid_t,
    local_sem,
    pair_s,
    pair_r,
    chain_s,
    chain_r,
    swap_s,
    swap_r,
    rows_s,
    rows_r,
    part_s,
    part_r,
    one_s,
    one_r,
):
    batches, tokens, width = top.shape
    half = width // 2
    chunks = pair_in.shape[0]
    chunk = pair_in.shape[3]
    cap = part_out.shape[2]
    rows = batches * cap
    flat = batches * tokens
    section = lax.axis_index("section")
    core = lax.axis_index("expert")
    shard = lax.axis_index("shard")
    low = lax.rem(section, 2)
    high = section // 2
    last = sections // 2 - 1
    partner = {"section": section + 1 - 2 * low}
    other_core = {"expert": 1 - core}
    other_shard = {"shard": 1 - shard}
    cols = part_out.shape[3]
    pieces = 4
    piece_depth = bh_v.shape[0] // pieces

    def columns(half_index, index):
        return pl.ds(pl.multiple_of(half_index * half + index * chunk, 128), chunk)

    small_loads = [
        pltpu.make_async_copy(source, target, local_sem.at[index])
        for index, (source, target) in enumerate(
            ((routes, routes_v), (probs, probs_v), (examples, examples_v))
        )
    ]
    own_load = pltpu.make_async_copy(
        branch.at[0, :, :, pl.ds(pl.multiple_of(low * half, 128), half)], own_v, local_sem.at[3]
    )
    hidden_load = pltpu.make_async_copy(hidden.at[0, 0], hidden_v, local_sem.at[4])
    top_load = pltpu.make_async_copy(top, top_v, local_sem.at[5])
    model_load = pltpu.make_async_copy(basis_model.at[0, 0], bm_v, local_sem.at[6])
    basis_load = pltpu.make_async_copy(basis_hidden.at[0, 0], bh_v, local_sem.at[7])
    for load in small_loads + [own_load]:
        load.start()

    barrier = pltpu.get_barrier_semaphore()
    for target in (partner, other_core, other_shard):
        pl.semaphore_signal(barrier, inc=1, device_id=target, device_id_type=MESH)

    @pl.when(high > 0)
    def _():
        pl.semaphore_signal(
            barrier, inc=1, device_id={"section": section - 2}, device_id_type=MESH
        )

    @pl.when(high < last)
    def _():
        pl.semaphore_signal(
            barrier, inc=1, device_id={"section": section + 2}, device_id_type=MESH
        )

    pl.semaphore_wait(
        barrier, 3 + jnp.where(high > 0, 1, 0) + jnp.where(high < last, 1, 0)
    )

    def remote(source, target, send, receive, device):
        return pltpu.make_async_remote_copy(
            src_ref=source,
            dst_ref=target,
            send_sem=send,
            recv_sem=receive,
            device_id=device,
            device_id_type=MESH,
        )

    def pair_copy(c):
        return remote(
            branch.at[0, :, :, columns(1 - low, c)],
            pair_in.at[c],
            pair_s.at[c],
            pair_r.at[c],
            partner,
        )

    def chain_copy(c):
        return remote(
            chain_out.at[c], chain_in.at[c], chain_s.at[c], chain_r.at[c],
            {"section": section - 2},
        )

    def swap_copy(c):
        return remote(swap_out.at[c], swap_in.at[c], swap_s.at[c], swap_r.at[c], partner)

    def rows_copy(c):
        return remote(
            rows_out.at[c], rows_all.at[core, c], rows_s.at[c], rows_r.at[c], other_core
        )

    def part_copy(m):
        return remote(part_out.at[m], part_in.at[m], part_s.at[m], part_r.at[m], other_shard)

    ex_copy = remote(ex_out, ex_all.at[core], one_s.at[0], one_r.at[0], other_core)
    hid_copy = remote(hid_own, hid_in, one_s.at[1], one_r.at[1], other_shard)

    for c in range(min(IN_FLIGHT, chunks)):
        pair_copy(c).start()
    hidden_load.start()
    basis_load.start()
    top_load.start()
    model_load.start()

    lane_token = lax.broadcasted_iota(jnp.int32, (tokens, tokens), 1)
    row_token = lax.broadcasted_iota(jnp.int32, (tokens, tokens), 0)
    slot_row = lax.broadcasted_iota(jnp.int32, (cap, tokens), 0).astype(jnp.float32)
    select_v[...] = jnp.zeros_like(select_v)
    for load in small_loads:
        load.wait()
    for m in range(batches):
        named = routes_v[0, m]
        weight = probs_v[0, m]
        example_row = examples_v[m].astype(jnp.float32)
        for place in range(2):
            expert = core if place == 0 else 1 - core
            hit = named == expert
            count_row = jnp.sum(jnp.where(hit, 1.0, 0.0), axis=0, keepdims=True)
            prob_row = jnp.sum(jnp.where(hit, weight, 0.0), axis=0, keepdims=True)
            count = jnp.sum(
                jnp.where(row_token == lane_token, count_row, 0.0), axis=1, keepdims=True
            )
            rank_row = jnp.sum(
                jnp.where(row_token < lane_token, count, 0.0), axis=0, keepdims=True
            )
            match = jnp.where(slot_row == rank_row, 1.0, 0.0) * count_row
            slot_prob = jnp.sum(match * prob_row, axis=1, keepdims=True)
            slot_example = jnp.sum(match * (example_row + 1.0), axis=1, keepdims=True) - 1.0
            first = place * rows + m * cap
            select_v[first : first + cap, m * tokens : (m + 1) * tokens] = match.astype(
                jnp.bfloat16
            )
            prob_v[first : first + cap, :] = jnp.broadcast_to(slot_prob, (cap, prob_v.shape[1]))
            wide = jnp.broadcast_to(slot_example.astype(jnp.int32), (cap, ex_out.shape[2]))
            if place == 0:
                ex_all[core, m] = wide
            else:
                ex_out[m] = wide
    ex_copy.start()

    @pl.when(high == last)
    def _():
        chain_in[...] = jnp.zeros_like(chain_in)

    own_load.wait()

    def feed(c):
        pair_copy(c).wait_send()

        @pl.when(c + IN_FLIGHT < chunks)
        def _():
            pair_copy(c + IN_FLIGHT).start()

    def carry(c):
        pair_copy(c).wait_recv()

        @pl.when(high < last)
        def _():
            chain_copy(c).wait_recv()

        own = own_v[:, :, pl.ds(pl.multiple_of(c * chunk, 128), chunk)].astype(jnp.float32)
        before = chain_in[c].astype(jnp.float32)

        @pl.when(high > 0)
        def _():
            total = before + own + pair_in[c].astype(jnp.float32)
            chain_out[c] = total.astype(jnp.bfloat16)
            chain_copy(c).start()

        swap_out[c] = (before + jnp.where(low == 1, own, 0.0)).astype(jnp.bfloat16)
        swap_copy(c).start()

    def rotate_hidden():
        hidden_load.wait()
        basis_load.wait()
        hid_own[...] = jnp.zeros_like(hid_own)

        def piece(p, _):
            acts = hidden_v[:, :, pl.ds(pl.multiple_of(p * piece_depth, 128), piece_depth)]
            hid_own[...] += jnp.dot(
                acts.reshape(batches * acts.shape[1], piece_depth),
                bh_v[pl.ds(pl.multiple_of(p * piece_depth, 128), piece_depth), :],
                preferred_element_type=jnp.float32,
            )
            return 0

        lax.fori_loop(0, pieces, piece, 0)
        hid_copy.start()

    def dispatch(c):
        swap_copy(c).wait_recv()
        select = select_v[...]
        pair_select = jnp.where(low == 0, select.astype(jnp.float32), 0.0).astype(jnp.bfloat16)
        slot_prob = prob_v[:, :1]

        def pick(matrix, block):
            return jnp.dot(
                matrix, block.reshape(flat, chunk), preferred_element_type=jnp.float32
            )

        mine = pick(select, top_v[:, :, columns(low, c)]) + pick(select, chain_in[c])
        mine = (mine + pick(pair_select, pair_in[c])) * slot_prob
        rest = pick(select, top_v[:, :, columns(1 - low, c)]) + pick(select, swap_in[c])
        rest = rest * slot_prob
        mine = mine.astype(jnp.bfloat16)
        rest = rest.astype(jnp.bfloat16)
        rows_out[c, low] = mine[rows:]
        rows_out[c, 1 - low] = rest[rows:]
        rows_copy(c).start()
        rows_all[core, c, low] = mine[:rows]
        rows_all[core, c, 1 - low] = rest[:rows]

    def rotate_model(c):
        rows_copy(c).wait_recv()
        total = None
        for h in range(2):
            term = jnp.dot(
                jnp.concatenate([rows_all[0, c, h], rows_all[1, c, h]], axis=0),
                bm_v[pl.ds(pl.multiple_of(h * half + c * chunk, 128), chunk), :],
                preferred_element_type=jnp.float32,
            )
            total = term if total is None else total + term

        @pl.when(c == 0)
        def _():
            model_sum[...] = total

        @pl.when(c > 0)
        def _():
            model_sum[...] += total

    def block_columns(index):
        return pl.ds(pl.multiple_of(index * cols, 128), cols)

    def squares(m):
        part_copy(m).wait_recv()
        blocks = []
        for owner in range(2):
            first = pl.ds(pl.multiple_of(owner * rows + m * cap, 16), cap)
            blocks.append(
                model_sum[first, block_columns(shard)]
                + part_in[m, owner].astype(jnp.float32)
            )
        total = None
        for owner in range(2):
            ids = ex_all[owner, m][:, :1]
            for q in range(SEQS):
                kept = jnp.where(ids == q, blocks[owner], 0.0)
                empty = jnp.zeros_like(kept)
                both = [kept, empty] if owner == 0 else [empty, kept]
                grad = jnp.dot(
                    hid_t[m],
                    jnp.concatenate(both, axis=0).astype(jnp.bfloat16),
                    preferred_element_type=jnp.float32,
                )
                total = grad * grad if total is None else total + grad * grad

        @pl.when(m == 0)
        def _():
            out[0, 0] = total

        @pl.when(m > 0)
        def _():
            out[0, 0] += total

    early = high < last - 1
    lag = jnp.minimum(chunks, 1 + 2 * high)

    @pl.when(high < last)
    def _():
        lax.fori_loop(0, chunks, lambda c, _: (feed(c), 0)[1], 0)

    @pl.when(early)
    def _():
        rotate_hidden()

    def step(k, _):
        @pl.when(k < chunks)
        def _():
            carry(k)

            @pl.when(high == last)
            def _():
                feed(k)

        @pl.when(jnp.logical_and(k == chunks - 1, jnp.logical_not(early)))
        def _():
            rotate_hidden()

        @pl.when(k == lag)
        def _():
            top_load.wait()
            model_load.wait()

        @pl.when(jnp.logical_and(k >= lag, k < chunks + lag))
        def _():
            dispatch(k - lag)

        @pl.when(k >= lag + 1)
        def _():
            rotate_model(k - lag - 1)

        return 0

    lax.fori_loop(0, chunks + lag + 1, step, 0)

    for m in range(batches):
        for owner in range(2):
            first = owner * rows + m * cap
            part_out[m, owner] = model_sum[
                first : first + cap, block_columns(1 - shard)
            ].astype(jnp.bfloat16)
        part_copy(m).start()
    ex_copy.wait_recv()
    hid_copy.wait_recv()
    turned = (hid_own[...] + hid_in[...]).T
    for m in range(batches):
        hid_t[m] = turned[:, 2 * m * cap : 2 * (m + 1) * cap].astype(jnp.bfloat16)
    lax.fori_loop(0, batches, lambda m, _: (squares(m), 0)[1], 0)
    out[...] = out[...] / (batches * 2 * SEQS)

    for c in range(chunks):
        swap_copy(c).wait_send()
        rows_copy(c).wait_send()
    for m in range(batches):
        part_copy(m).wait_send()
    ex_copy.wait_send()
    hid_copy.wait_send()

    @pl.when(high > 0)
    def _():
        for c in range(chunks):
            chain_copy(c).wait_send()


def on_device(
    routes,
    route_probs,
    example_ids,
    top_cotangent,
    branch_cotangent,
    hidden_acts,
    basis_hidden,
    basis_model,
):
    sections = lax.axis_size("section")
    shards = lax.axis_size("shard")
    batches, tokens, width = top_cotangent.shape
    slots, depth = hidden_acts.shape[3:]
    cap = slots // lax.axis_size("expert")
    rank_hidden = basis_hidden.shape[3]
    cols = basis_model.shape[3] // shards
    half = width // 2
    chunk = CHUNK if half % CHUNK == 0 else 128
    chunks = half // chunk
    bf16, f32 = jnp.bfloat16, jnp.float32
    vmem = pl.BlockSpec(memory_space=pltpu.VMEM)
    hbm = pl.BlockSpec(memory_space=pl.ANY)
    dma = pltpu.SemaphoreType.DMA
    moving = pltpu.VMEM((chunks, batches, tokens, chunk), bf16)
    routes = jnp.swapaxes(routes, 2, 3)
    route_probs = jnp.swapaxes(route_probs, 2, 3)
    flops = 2 * batches * slots * (depth * rank_hidden + width * cols * shards)
    return pl.pallas_call(
        functools.partial(kernel, sections),
        out_shape=jax.ShapeDtypeStruct((1, 1, rank_hidden, cols), f32),
        in_specs=[hbm] * 8,
        out_specs=vmem,
        scratch_shapes=[
            pltpu.VMEM(routes.shape, jnp.int32),
            pltpu.VMEM(route_probs.shape, f32),
            pltpu.VMEM(example_ids.shape, jnp.int32),
            pltpu.VMEM((batches, tokens, width), bf16),
            pltpu.VMEM((batches, tokens, half), bf16),
            pltpu.VMEM((batches, slots, depth), bf16),
            pltpu.VMEM((depth, rank_hidden), bf16),
            pltpu.VMEM((width, cols * shards), bf16),
            moving,
            moving,
            moving,
            moving,
            moving,
            pltpu.VMEM((2 * batches * cap, batches * tokens), bf16),
            pltpu.VMEM((2 * batches * cap, 128), f32),
            pltpu.VMEM((batches, cap, 128), jnp.int32),
            pltpu.VMEM((2, batches, cap, 128), jnp.int32),
            pltpu.VMEM((chunks, 2, batches * cap, chunk), bf16),
            pltpu.VMEM((2, chunks, 2, batches * cap, chunk), bf16),
            pltpu.VMEM((batches * slots, cols * shards), f32),
            pltpu.VMEM((batches, 2, cap, cols), bf16),
            pltpu.VMEM((batches, 2, cap, cols), bf16),
            pltpu.VMEM((batches * slots, rank_hidden), f32),
            pltpu.VMEM((batches * slots, rank_hidden), f32),
            pltpu.VMEM((batches, rank_hidden, slots), bf16),
            dma((8,)),
        ]
        + [dma((chunks,))] * 8
        + [dma((batches,))] * 2
        + [dma((2,))] * 2,
        compiler_params=pltpu.CompilerParams(
            collective_id=0, has_side_effects=True, vmem_limit_bytes=60 * 1024 * 1024
        ),
        cost_estimate=pl.CostEstimate(
            flops=flops, bytes_accessed=16 * 1024 * 1024, transcendentals=0
        ),
    )(
        routes,
        route_probs,
        example_ids,
        top_cotangent,
        branch_cotangent,
        hidden_acts,
        basis_hidden,
        basis_model,
    )


def solution(mesh):
    return jax.shard_map(
        on_device,
        mesh=mesh,
        in_specs=(
            P("section", None, "expert", None),
            P("section", None, "expert", None),
            P(None, "expert", None),
            P(None, "expert", "shard"),
            P("section", None, "expert", "shard"),
            P("section", "expert", None, None, "shard"),
            P("section", "expert", "shard", None),
            P("section", "expert", "shard", None),
        ),
        out_specs=P("section", "expert", None, "shard"),
        check_vma=False,
    )
```

time: 51.3 us -> 43.9 us (0.86)
  local copies, waits for them, and re-layouts: 6.9 us -> 1.87 us
  Pallas kernels: 44.1 us -> 41.8 us
    unnamed x11 -> x1, local copies, waits for them, and re-layouts: 6.9 us -> 1.87 us
    pallas_call x1, Pallas kernels: 44.1 us -> 41.8 us  [on_device(): pl.pallas_call(functools.partial(kernel, sections), out_shape=jax.ShapeDt...]
where the time goes in v2:
time: 43.9 us; the launch traced here: 43.7 us
  Pallas kernels  41.8 us (95%)
  local copies, waits for them, and re-layouts  1.87 us (4%)
    pallas_call x1, Pallas kernels, on_device(): pl.pallas_call(functools.partial(kernel, sections), out_shape=jax.ShapeDt...  41.8 us
    unnamed x1, local copies, waits for them, and re-layouts  1.87 us

profile of v2, /device:TPU:0, one launch (start us, length us, event | category | flops | bytes accessed | tf_op | source)
XLA Modules:
  0.0 43.7 jit_solution(2569520279856622921)
XLA Ops:
  0.0 41.8 %shard_map.82 = f32[1,1,256,512]{3,2,1,0:T(8,128)} custom-call(s32[1,4,2,32]{3,2,1,0:T(2,128)} %bitcast.2, f32[1,4,2,32]{3,2,1,0:T(2,128)} %bitcast.3, s32[4,1,32]{2,1,0:T(1,128)} %examples.1, bf16[4,32,3072]{2,1,0:T(8,128)(2,1)} %top.1, bf16[1,4,32,3072]{3,2,1,0:T(8,128)(2,1)} %branch.1, bf16[1,1,4,32,8192]{4,3,2,1,0:T(8,128)(2,1)} %hidden.1, ...), custom_call_target="tpu_custom_call" | custom-call | flops 1342177280 | bytes 16777216 | tf_op jit(solution)/shard_map/pallas_call | solution.py:430
  41.9 1.9 %copy.10 = f32[1,1,256,512]{3,2,1,0:T(8,128)} copy(f32[1,1,256,512]{3,2,1,0:T(8,128)} %shard_map.82) | data formatting | bytes 1048576

commit v3 on v2

--- a/solution.py
+++ b/solution.py
@@ -10,6 +10,9 @@
 SEQS = 2
 CHUNK = 256
 IN_FLIGHT = 3
+SWAP_LAG = 2
+ROWS_LAG = 2
+HOP_LAG = 2
 MESH = pl.DeviceIdType.MESH
 
 
@@ -234,7 +237,6 @@
             chain_copy(c).start()
 
         swap_out[c] = (before + jnp.where(low == 1, own, 0.0)).astype(jnp.bfloat16)
-        swap_copy(c).start()
 
     def rotate_hidden():
         hidden_load.wait()
@@ -330,7 +332,9 @@
             out[0, 0] += total
 
     early = high < last - 1
-    lag = jnp.minimum(chunks, 1 + 2 * high)
+    held = jnp.minimum(chunks - 1, HOP_LAG * high)
+    lag = held + SWAP_LAG
+    model_lag = lag + ROWS_LAG
 
     @pl.when(high < last)
     def _():
@@ -353,6 +357,10 @@
         def _():
             rotate_hidden()
 
+        @pl.when(jnp.logical_and(k >= held, k < chunks + held))
+        def _():
+            swap_copy(k - held).start()
+
         @pl.when(k == lag)
         def _():
             top_load.wait()
@@ -362,13 +370,13 @@
         def _():
             dispatch(k - lag)
 
-        @pl.when(k >= lag + 1)
-        def _():
-            rotate_model(k - lag - 1)
+        @pl.when(k >= model_lag)
+        def _():
+            rotate_model(k - model_lag)
 
         return 0
 
-    lax.fori_loop(0, chunks + lag + 1, step, 0)
+    lax.fori_loop(0, chunks + model_lag, step, 0)
 
     for m in range(batches):
         for owner in range(2):
@@ -383,7 +391,6 @@
     for m in range(batches):
         hid_t[m] = turned[:, 2 * m * cap : 2 * (m + 1) * cap].astype(jnp.bfloat16)
     lax.fori_loop(0, batches, lambda m, _: (squares(m), 0)[1], 0)
-    out[...] = out[...] / (batches * 2 * SEQS)
 
     for c in range(chunks):
         swap_copy(c).wait_send()
@@ -427,7 +434,7 @@
     routes = jnp.swapaxes(routes, 2, 3)
     route_probs = jnp.swapaxes(route_probs, 2, 3)
     flops = 2 * batches * slots * (depth * rank_hidden + width * cols * shards)
-    return pl.pallas_call(
+    square_sum = pl.pallas_call(
         functools.partial(kernel, sections),
         out_shape=jax.ShapeDtypeStruct((1, 1, rank_hidden, cols), f32),
         in_specs=[hbm] * 8,
@@ -479,6 +486,7 @@
         basis_hidden,
         basis_model,
     )
+    return square_sum / (batches * lax.axis_size("expert") * SEQS)
 
 
 def solution(mesh):

time: 43.9 us -> 41.8 us (0.952)
  Pallas kernels: 41.8 us -> 39.8 us
  other arithmetic: 0 us -> 1.88 us
  local copies, waits for them, and re-layouts: 1.87 us -> 0 us
    pallas_call x1, Pallas kernels: 41.8 us -> 39.8 us  [on_device(): pl.pallas_call(functools.partial(kernel, sections), out_shape=jax.ShapeDt...]
    div x0 -> x1, other arithmetic: none -> 1.88 us  [on_device(): return square_sum / (batches * lax.axis_size('expert') * SEQS)]
    unnamed x1 -> x0, local copies, waits for them, and re-layouts: 1.87 us -> none
where the time goes in v3:
time: 41.8 us; the launch traced here: 41.7 us
  Pallas kernels  39.8 us (95%)
  other arithmetic  1.88 us (4%)
    pallas_call x1, Pallas kernels, on_device(): pl.pallas_call(functools.partial(kernel, sections), out_shape=jax.ShapeDt...  39.8 us
    div x1, other arithmetic, on_device(): return square_sum / (batches * lax.axis_size('expert') * SEQS)  1.88 us

profile of v3, /device:TPU:0, one launch (start us, length us, event | category | flops | bytes accessed | tf_op | source)
XLA Modules:
  0.0 41.7 jit_solution(9043140239966807834)
XLA Ops:
  0.0 39.8 %shard_map.82 = f32[1,1,256,512]{3,2,1,0:T(8,128)} custom-call(s32[1,4,2,32]{3,2,1,0:T(2,128)} %bitcast.2, f32[1,4,2,32]{3,2,1,0:T(2,128)} %bitcast.3, s32[4,1,32]{2,1,0:T(1,128)} %examples.1, bf16[4,32,3072]{2,1,0:T(8,128)(2,1)} %top.1, bf16[1,4,32,3072]{3,2,1,0:T(8,128)(2,1)} %branch.1, bf16[1,1,4,32,8192]{4,3,2,1,0:T(8,128)(2,1)} %hidden.1, ...), custom_call_target="tpu_custom_call" | custom-call | flops 1342177280 | bytes 16777216 | tf_op jit(solution)/shard_map/pallas_call | solution.py:437
  39.8 1.9 %broadcast_multiply_fusion = f32[1,1,256,512]{3,2,1,0:T(8,128)} fusion(f32[1,1,256,512]{3,2,1,0:T(8,128)} %shard_map.82), kind=kLoop, calls=%fused_computation | loop fusion | flops 131072 | bytes 1048576 | tf_op jit(solution)/shard_map/div | solution.py:489

commit v4 on v3

--- a/solution.py
+++ b/solution.py
@@ -85,6 +85,7 @@
     cols = part_out.shape[3]
     pieces = 4
     piece_depth = bh_v.shape[0] // pieces
+    group = batches // hid_t.shape[0]
 
     def columns(half_index, index):
         return pl.ds(pl.multiple_of(half_index * half + index * chunk, 128), chunk)
@@ -196,9 +197,8 @@
             slot_prob = jnp.sum(match * prob_row, axis=1, keepdims=True)
             slot_example = jnp.sum(match * (example_row + 1.0), axis=1, keepdims=True) - 1.0
             first = place * rows + m * cap
-            select_v[first : first + cap, m * tokens : (m + 1) * tokens] = match.astype(
-                jnp.bfloat16
-            )
+            for at in (m * tokens, flat + m * tokens):
+                select_v[first : first + cap, at : at + tokens] = match.astype(jnp.bfloat16)
             prob_v[first : first + cap, :] = jnp.broadcast_to(slot_prob, (cap, prob_v.shape[1]))
             wide = jnp.broadcast_to(slot_example.astype(jnp.int32), (cap, ex_out.shape[2]))
             if place == 0:
@@ -258,20 +258,25 @@
     def dispatch(c):
         swap_copy(c).wait_recv()
         select = select_v[...]
-        pair_select = jnp.where(low == 0, select.astype(jnp.float32), 0.0).astype(jnp.bfloat16)
         slot_prob = prob_v[:, :1]
 
-        def pick(matrix, block):
-            return jnp.dot(
-                matrix, block.reshape(flat, chunk), preferred_element_type=jnp.float32
+        def picked(cotangent):
+            wide = cotangent.reshape(flat, chunk)
+            coarse = wide.astype(jnp.bfloat16)
+            fine = (wide - coarse.astype(jnp.float32)).astype(jnp.bfloat16)
+            found = jnp.dot(
+                select,
+                jnp.concatenate([coarse, fine], axis=0),
+                preferred_element_type=jnp.float32,
             )
-
-        mine = pick(select, top_v[:, :, columns(low, c)]) + pick(select, chain_in[c])
-        mine = (mine + pick(pair_select, pair_in[c])) * slot_prob
-        rest = pick(select, top_v[:, :, columns(1 - low, c)]) + pick(select, swap_in[c])
-        rest = rest * slot_prob
-        mine = mine.astype(jnp.bfloat16)
-        rest = rest.astype(jnp.bfloat16)
+            return (found * slot_prob).astype(jnp.bfloat16)
+
+        def wide_top(half_index):
+            return top_v[:, :, columns(half_index, c)].astype(jnp.float32)
+
+        pair_term = jnp.where(low == 0, pair_in[c].astype(jnp.float32), 0.0)
+        mine = picked(wide_top(low) + chain_in[c].astype(jnp.float32) + pair_term)
+        rest = picked(wide_top(1 - low) + swap_in[c].astype(jnp.float32))
         rows_out[c, low] = mine[rows:]
         rows_out[c, 1 - low] = rest[rows:]
         rows_copy(c).start()
@@ -280,14 +285,23 @@
 
     def rotate_model(c):
         rows_copy(c).wait_recv()
-        total = None
-        for h in range(2):
-            term = jnp.dot(
-                jnp.concatenate([rows_all[0, c, h], rows_all[1, c, h]], axis=0),
-                bm_v[pl.ds(pl.multiple_of(h * half + c * chunk, 128), chunk), :],
-                preferred_element_type=jnp.float32,
-            )
-            total = term if total is None else total + term
+        total = jnp.dot(
+            jnp.concatenate(
+                [
+                    jnp.concatenate([rows_all[0, c, h], rows_all[1, c, h]], axis=0)
+                    for h in range(2)
+                ],
+                axis=1,
+            ),
+            jnp.concatenate(
+                [
+                    bm_v[pl.ds(pl.multiple_of(h * half + c * chunk, 128), chunk), :]
+                    for h in range(2)
+                ],
+                axis=0,
+            ),
+            preferred_element_type=jnp.float32,
+        )
 
         @pl.when(c == 0)
         def _():
@@ -300,49 +314,69 @@
     def block_columns(index):
         return pl.ds(pl.multiple_of(index * cols, 128), cols)
 
-    def squares(m):
-        part_copy(m).wait_recv()
+    turns = cap // 2 + 1
+
+    def padding(like):
+        return [jnp.zeros((hid_t.shape[2] - group * 2 * turns * cap, like.shape[1]), jnp.float32)]
+
+    def prepare_hidden():
+        ex_copy.wait_recv()
+        hid_copy.wait_recv()
+        hid = (hid_own[...] + hid_in[...]).astype(jnp.bfloat16).astype(jnp.float32)
+        for part in range(batches // group):
+            blocks = []
+            for m in range(part * group, (part + 1) * group):
+                for owner in range(2):
+                    first = m * 2 * cap + owner * cap
+                    block = hid[first : first + cap]
+                    ids = ex_all[owner, m].astype(jnp.float32)
+                    for turn in range(turns):
+                        share = 1.0 if turn in (0, cap // 2) else 2.0
+                        if turn:
+                            other = pltpu.roll(block, turn, 0)
+                            other_ids = pltpu.roll(ids, turn, 0)
+                        else:
+                            other, other_ids = block, ids
+                        same = jnp.where(ids == other_ids, share, 0.0)
+                        blocks.append(block * other * same[:, :1])
+            pairs = jnp.concatenate(blocks + padding(hid), axis=0)
+            hid_t[part] = pairs.T.astype(jnp.bfloat16)
+
+    def squares(part):
         blocks = []
-        for owner in range(2):
-            first = pl.ds(pl.multiple_of(owner * rows + m * cap, 16), cap)
-            blocks.append(
-                model_sum[first, block_columns(shard)]
-                + part_in[m, owner].astype(jnp.float32)
-            )
-        total = None
-        for owner in range(2):
-            ids = ex_all[owner, m][:, :1]
-            for q in range(SEQS):
-                kept = jnp.where(ids == q, blocks[owner], 0.0)
-                empty = jnp.zeros_like(kept)
-                both = [kept, empty] if owner == 0 else [empty, kept]
-                grad = jnp.dot(
-                    hid_t[m],
-                    jnp.concatenate(both, axis=0).astype(jnp.bfloat16),
-                    preferred_element_type=jnp.float32,
-                )
-                total = grad * grad if total is None else total + grad * grad
-
-        @pl.when(m == 0)
-        def _():
-            out[0, 0] = total
-
-        @pl.when(m > 0)
-        def _():
-            out[0, 0] += total
+        for m in range(part * group, (part + 1) * group):
+            part_copy(m).wait_recv()
+            for owner in range(2):
+                first = owner * rows + m * cap
+                block = model_sum[first : first + cap, block_columns(shard)]
+                block = block + part_in[m, owner].astype(jnp.float32)
+                block = block.astype(jnp.bfloat16).astype(jnp.float32)
+                for turn in range(turns):
+                    other = pltpu.roll(block, turn, 0) if turn else block
+                    blocks.append(block * other)
+        pairs = jnp.concatenate(blocks + padding(blocks[0]), axis=0).astype(jnp.bfloat16)
+        return jnp.dot(hid_t[part], pairs, preferred_element_type=jnp.float32)
 
     early = high < last - 1
     held = jnp.minimum(chunks - 1, HOP_LAG * high)
     lag = held + SWAP_LAG
     model_lag = lag + ROWS_LAG
 
+    @pl.when(early)
+    def _():
+        rotate_hidden()
+
     @pl.when(high < last)
     def _():
         lax.fori_loop(0, chunks, lambda c, _: (feed(c), 0)[1], 0)
 
-    @pl.when(early)
-    def _():
-        rotate_hidden()
+    @pl.when(high == 0)
+    def _():
+        @pl.when(jnp.logical_not(early))
+        def _():
+            rotate_hidden()
+
+        prepare_hidden()
 
     def step(k, _):
         @pl.when(k < chunks)
@@ -355,7 +389,13 @@
 
         @pl.when(jnp.logical_and(k == chunks - 1, jnp.logical_not(early)))
         def _():
-            rotate_hidden()
+            @pl.when(high > 0)
+            def _():
+                rotate_hidden()
+
+        @pl.when(jnp.logical_and(k == chunks + 1, high > 0))
+        def _():
+            prepare_hidden()
 
         @pl.when(jnp.logical_and(k >= held, k < chunks + held))
         def _():
@@ -385,12 +425,9 @@
                 first : first + cap, block_columns(1 - shard)
             ].astype(jnp.bfloat16)
         part_copy(m).start()
-    ex_copy.wait_recv()
-    hid_copy.wait_recv()
-    turned = (hid_own[...] + hid_in[...]).T
-    for m in range(batches):
-        hid_t[m] = turned[:, 2 * m * cap : 2 * (m + 1) * cap].astype(jnp.bfloat16)
-    lax.fori_loop(0, batches, lambda m, _: (squares(m), 0)[1], 0)
+    out[0, 0] = squares(0)
+    for part in range(1, batches // group):
+        out[0, 0] += squares(part)
 
     for c in range(chunks):
         swap_copy(c).wait_send()
@@ -426,6 +463,8 @@
     half = width // 2
     chunk = CHUNK if half % CHUNK == 0 else 128
     chunks = half // chunk
+    group = 2 if batches % 2 == 0 else 1
+    pairs = -(-group * 2 * (cap // 2 + 1) * cap // 128) * 128
     bf16, f32 = jnp.bfloat16, jnp.float32
     vmem = pl.BlockSpec(memory_space=pltpu.VMEM)
     hbm = pl.BlockSpec(memory_space=pl.ANY)
@@ -453,7 +492,7 @@
             moving,
             moving,
             moving,
-            pltpu.VMEM((2 * batches * cap, batches * tokens), bf16),
+            pltpu.VMEM((2 * batches * cap, 2 * batches * tokens), bf16),
             pltpu.VMEM((2 * batches * cap, 128), f32),
             pltpu.VMEM((batches, cap, 128), jnp.int32),
             pltpu.VMEM((2, batches, cap, 128), jnp.int32),
@@ -464,7 +503,7 @@
             pltpu.VMEM((batches, 2, cap, cols), bf16),
             pltpu.VMEM((batches * slots, rank_hidden), f32),
             pltpu.VMEM((batches * slots, rank_hidden), f32),
-            pltpu.VMEM((batches, rank_hidden, slots), bf16),
+            pltpu.VMEM((batches // group, rank_hidden, pairs), bf16),
             dma((8,)),
         ]
         + [dma((chunks,))] * 8

time: 41.8 us -> 41.6 us (level)
  no operation moved by 1% of the time
where the time goes in v4:
time: 41.6 us; the launch traced here: 41.5 us
  Pallas kernels  39.6 us (95%)
  other arithmetic  1.88 us (5%)
    pallas_call x1, Pallas kernels, on_device(): pl.pallas_call(functools.partial(kernel, sections), out_shape=jax.ShapeDt...  39.6 us
    div x1, other arithmetic, on_device(): return square_sum / (batches * lax.axis_size('expert') * SEQS)  1.88 us

profile of v4, /device:TPU:0, one launch (start us, length us, event | category | flops | bytes accessed | tf_op | source)
XLA Modules:
  0.0 41.5 jit_solution(8252310298984763943)
XLA Ops:
  0.0 39.6 %shard_map.82 = f32[1,1,256,512]{3,2,1,0:T(8,128)} custom-call(s32[1,4,2,32]{3,2,1,0:T(2,128)} %bitcast.2, f32[1,4,2,32]{3,2,1,0:T(2,128)} %bitcast.3, s32[4,1,32]{2,1,0:T(1,128)} %examples.1, bf16[4,32,3072]{2,1,0:T(8,128)(2,1)} %top.1, bf16[1,4,32,3072]{3,2,1,0:T(8,128)(2,1)} %branch.1, bf16[1,1,4,32,8192]{4,3,2,1,0:T(8,128)(2,1)} %hidden.1, ...), custom_call_target="tpu_custom_call" | custom-call | flops 1342177280 | bytes 16777216 | tf_op jit(solution)/shard_map/pallas_call | solution.py:476
  39.6 1.9 %broadcast_multiply_fusion = f32[1,1,256,512]{3,2,1,0:T(8,128)} fusion(f32[1,1,256,512]{3,2,1,0:T(8,128)} %shard_map.82), kind=kLoop, calls=%fused_computation | loop fusion | flops 131072 | bytes 1048576 | tf_op jit(solution)/shard_map/div | solution.py:528

commit v5 on v4

--- a/solution.py
+++ b/solution.py
@@ -32,6 +32,7 @@
     examples_v,
     top_v,
     own_v,
+    stage_v,
     hidden_v,
     bh_v,
     bm_v,
@@ -53,6 +54,7 @@
     hid_in,
     hid_t,
     local_sem,
+    stage_sem,
     pair_s,
     pair_r,
     chain_s,
@@ -103,6 +105,14 @@
     top_load = pltpu.make_async_copy(top, top_v, local_sem.at[5])
     model_load = pltpu.make_async_copy(basis_model.at[0, 0], bm_v, local_sem.at[6])
     basis_load = pltpu.make_async_copy(basis_hidden.at[0, 0], bh_v, local_sem.at[7])
+
+    def stage_load(c):
+        return pltpu.make_async_copy(
+            branch.at[0, :, :, columns(1 - low, c)], stage_v.at[c], stage_sem.at[c]
+        )
+
+    for c in range(chunks):
+        stage_load(c).start()
     for load in small_loads + [own_load]:
         load.start()
 
@@ -138,7 +148,7 @@
 
     def pair_copy(c):
         return remote(
-            branch.at[0, :, :, columns(1 - low, c)],
+            stage_v.at[c],
             pair_in.at[c],
             pair_s.at[c],
             pair_r.at[c],
@@ -166,6 +176,7 @@
     hid_copy = remote(hid_own, hid_in, one_s.at[1], one_r.at[1], other_shard)
 
     for c in range(min(IN_FLIGHT, chunks)):
+        stage_load(c).wait()
         pair_copy(c).start()
     hidden_load.start()
     basis_load.start()
@@ -214,10 +225,10 @@
     own_load.wait()
 
     def feed(c):
-        pair_copy(c).wait_send()
-
         @pl.when(c + IN_FLIGHT < chunks)
         def _():
+            pair_copy(c).wait_send()
+            stage_load(c + IN_FLIGHT).wait()
             pair_copy(c + IN_FLIGHT).start()
 
     def carry(c):
@@ -359,7 +370,7 @@
 
     early = high < last - 1
     held = jnp.minimum(chunks - 1, HOP_LAG * high)
-    lag = held + SWAP_LAG
+    lag = jnp.where(high > 0, jnp.maximum(chunks, held + SWAP_LAG), held + SWAP_LAG)
     model_lag = lag + ROWS_LAG
 
     @pl.when(early)
@@ -375,8 +386,6 @@
         @pl.when(jnp.logical_not(early))
         def _():
             rotate_hidden()
-
-        prepare_hidden()
 
     def step(k, _):
         @pl.when(k < chunks)
@@ -387,19 +396,19 @@
             def _():
                 feed(k)
 
+        @pl.when(jnp.logical_and(k >= held, k < chunks + held))
+        def _():
+            swap_copy(k - held).start()
+
         @pl.when(jnp.logical_and(k == chunks - 1, jnp.logical_not(early)))
         def _():
             @pl.when(high > 0)
             def _():
                 rotate_hidden()
 
-        @pl.when(jnp.logical_and(k == chunks + 1, high > 0))
+        @pl.when(k == jnp.where(high > 0, chunks + 1, chunks // 2))
         def _():
             prepare_hidden()
-
-        @pl.when(jnp.logical_and(k >= held, k < chunks + held))
-        def _():
-            swap_copy(k - held).start()
 
         @pl.when(k == lag)
         def _():
@@ -432,6 +441,8 @@
     for c in range(chunks):
         swap_copy(c).wait_send()
         rows_copy(c).wait_send()
+    for c in range(max(chunks - IN_FLIGHT, 0), chunks):
+        pair_copy(c).wait_send()
     for m in range(batches):
         part_copy(m).wait_send()
     ex_copy.wait_send()
@@ -484,6 +495,7 @@
             pltpu.VMEM(example_ids.shape, jnp.int32),
             pltpu.VMEM((batches, tokens, width), bf16),
             pltpu.VMEM((batches, tokens, half), bf16),
+            moving,
             pltpu.VMEM((batches, slots, depth), bf16),
             pltpu.VMEM((depth, rank_hidden), bf16),
             pltpu.VMEM((width, cols * shards), bf16),
@@ -506,7 +518,7 @@
             pltpu.VMEM((batches // group, rank_hidden, pairs), bf16),
             dma((8,)),
         ]
-        + [dma((chunks,))] * 8
+        + [dma((chunks,))] * 9
         + [dma((batches,))] * 2
         + [dma((2,))] * 2,
         compiler_params=pltpu.CompilerParams(

time: 41.6 us -> 40.3 us (0.969)
  Pallas kernels: 39.6 us -> 38.2 us
    pallas_call x1, Pallas kernels: 39.6 us -> 38.2 us  [on_device(): pl.pallas_call(functools.partial(kernel, sections), out_shape=jax.ShapeDt...]
where the time goes in v5:
time: 40.3 us; the launch traced here: 40.1 us
  Pallas kernels  38.2 us (95%)
  other arithmetic  1.88 us (5%)
    pallas_call x1, Pallas kernels, on_device(): pl.pallas_call(functools.partial(kernel, sections), out_shape=jax.ShapeDt...  38.2 us
    div x1, other arithmetic, on_device(): return square_sum / (batches * lax.axis_size('expert') * SEQS)  1.88 us

profile of v5, /device:TPU:0, one launch (start us, length us, event | category | flops | bytes accessed | tf_op | source)
XLA Modules:
  0.0 40.1 jit_solution(6592331586787342242)
XLA Ops:
  0.0 38.2 %shard_map.82 = f32[1,1,256,512]{3,2,1,0:T(8,128)} custom-call(s32[1,4,2,32]{3,2,1,0:T(2,128)} %bitcast.2, f32[1,4,2,32]{3,2,1,0:T(2,128)} %bitcast.3, s32[4,1,32]{2,1,0:T(1,128)} %examples.1, bf16[4,32,3072]{2,1,0:T(8,128)(2,1)} %top.1, bf16[1,4,32,3072]{3,2,1,0:T(8,128)(2,1)} %branch.1, bf16[1,1,4,32,8192]{4,3,2,1,0:T(8,128)(2,1)} %hidden.1, ...), custom_call_target="tpu_custom_call" | custom-call | flops 1342177280 | bytes 16777216 | tf_op jit(solution)/shard_map/pallas_call | solution.py:487
  38.2 1.9 %broadcast_multiply_fusion = f32[1,1,256,512]{3,2,1,0:T(8,128)} fusion(f32[1,1,256,512]{3,2,1,0:T(8,128)} %shard_map.82), kind=kLoop, calls=%fused_computation | loop fusion | flops 131072 | bytes 1048576 | tf_op jit(solution)/shard_map/div | solution.py:540

commit v6 on v5

--- a/solution.py
+++ b/solution.py
@@ -8,11 +8,11 @@
 from jax.sharding import PartitionSpec as P
 
 SEQS = 2
-CHUNK = 256
-IN_FLIGHT = 3
-SWAP_LAG = 2
+CHUNK = 128
+IN_FLIGHT = 4
+SWAP_LAG = 3
 ROWS_LAG = 2
-HOP_LAG = 2
+HOP_LAG = 3
 MESH = pl.DeviceIdType.MESH
 
 
@@ -183,40 +183,45 @@
     top_load.start()
     model_load.start()
 
-    lane_token = lax.broadcasted_iota(jnp.int32, (tokens, tokens), 1)
-    row_token = lax.broadcasted_iota(jnp.int32, (tokens, tokens), 0)
-    slot_row = lax.broadcasted_iota(jnp.int32, (cap, tokens), 0).astype(jnp.float32)
-    select_v[...] = jnp.zeros_like(select_v)
-    for load in small_loads:
-        load.wait()
-    for m in range(batches):
-        named = routes_v[0, m]
-        weight = probs_v[0, m]
-        example_row = examples_v[m].astype(jnp.float32)
-        for place in range(2):
-            expert = core if place == 0 else 1 - core
-            hit = named == expert
-            count_row = jnp.sum(jnp.where(hit, 1.0, 0.0), axis=0, keepdims=True)
-            prob_row = jnp.sum(jnp.where(hit, weight, 0.0), axis=0, keepdims=True)
-            count = jnp.sum(
-                jnp.where(row_token == lane_token, count_row, 0.0), axis=1, keepdims=True
-            )
-            rank_row = jnp.sum(
-                jnp.where(row_token < lane_token, count, 0.0), axis=0, keepdims=True
-            )
-            match = jnp.where(slot_row == rank_row, 1.0, 0.0) * count_row
-            slot_prob = jnp.sum(match * prob_row, axis=1, keepdims=True)
-            slot_example = jnp.sum(match * (example_row + 1.0), axis=1, keepdims=True) - 1.0
-            first = place * rows + m * cap
-            for at in (m * tokens, flat + m * tokens):
-                select_v[first : first + cap, at : at + tokens] = match.astype(jnp.bfloat16)
-            prob_v[first : first + cap, :] = jnp.broadcast_to(slot_prob, (cap, prob_v.shape[1]))
-            wide = jnp.broadcast_to(slot_example.astype(jnp.int32), (cap, ex_out.shape[2]))
-            if place == 0:
-                ex_all[core, m] = wide
-            else:
-                ex_out[m] = wide
-    ex_copy.start()
+    def slot_tables():
+        lane_token = lax.broadcasted_iota(jnp.int32, (tokens, tokens), 1)
+        row_token = lax.broadcasted_iota(jnp.int32, (tokens, tokens), 0)
+        slot_row = lax.broadcasted_iota(jnp.int32, (cap, tokens), 0).astype(jnp.float32)
+        select_v[...] = jnp.zeros_like(select_v)
+        for load in small_loads:
+            load.wait()
+        for m in range(batches):
+            named = routes_v[0, m]
+            weight = probs_v[0, m]
+            example_row = examples_v[m].astype(jnp.float32)
+            for place in range(2):
+                expert = core if place == 0 else 1 - core
+                hit = named == expert
+                count_row = jnp.sum(jnp.where(hit, 1.0, 0.0), axis=0, keepdims=True)
+                prob_row = jnp.sum(jnp.where(hit, weight, 0.0), axis=0, keepdims=True)
+                count = jnp.sum(
+                    jnp.where(row_token == lane_token, count_row, 0.0), axis=1, keepdims=True
+                )
+                rank_row = jnp.sum(
+                    jnp.where(row_token < lane_token, count, 0.0), axis=0, keepdims=True
+                )
+                match = jnp.where(slot_row == rank_row, 1.0, 0.0) * count_row
+                slot_prob = jnp.sum(match * prob_row, axis=1, keepdims=True)
+                slot_example = jnp.sum(match * (example_row + 1.0), axis=1, keepdims=True) - 1.0
+                first = place * rows + m * cap
+                for at in (m * tokens, flat + m * tokens):
+                    select_v[first : first + cap, at : at + tokens] = match.astype(jnp.bfloat16)
+                prob_v[first : first + cap, :] = jnp.broadcast_to(slot_prob, (cap, prob_v.shape[1]))
+                wide = jnp.broadcast_to(slot_example.astype(jnp.int32), (cap, ex_out.shape[2]))
+                if place == 0:
+                    ex_all[core, m] = wide
+                else:
+                    ex_out[m] = wide
+        ex_copy.start()
+
+    @pl.when(high < last)
+    def _():
+        slot_tables()
 
     @pl.when(high == last)
     def _():
@@ -399,6 +404,10 @@
         @pl.when(jnp.logical_and(k >= held, k < chunks + held))
         def _():
             swap_copy(k - held).start()
+
+        @pl.when(jnp.logical_and(k == chunks - 1, high == last))
+        def _():
+            slot_tables()
 
         @pl.when(jnp.logical_and(k == chunks - 1, jnp.logical_not(early)))
         def _():

time: 40.3 us -> 41.1 us (1.020)
  Pallas kernels: 38.2 us -> 39 us
    pallas_call x1, Pallas kernels: 38.2 us -> 39 us  [on_device(): pl.pallas_call(functools.partial(kernel, sections), out_shape=jax.ShapeDt...]
where the time goes in v6:
time: 41.1 us; the launch traced here: 40.9 us
  Pallas kernels  39 us (95%)
  other arithmetic  1.88 us (5%)
    pallas_call x1, Pallas kernels, on_device(): pl.pallas_call(functools.partial(kernel, sections), out_shape=jax.ShapeDt...  39 us
    div x1, other arithmetic, on_device(): return square_sum / (batches * lax.axis_size('expert') * SEQS)  1.88 us

profile of v6, /device:TPU:0, one launch (start us, length us, event | category | flops | bytes accessed | tf_op | source)
XLA Modules:
  0.0 40.9 jit_solution(17156484215137663963)
XLA Ops:
  0.0 39.0 %shard_map.82 = f32[1,1,256,512]{3,2,1,0:T(8,128)} custom-call(s32[1,4,2,32]{3,2,1,0:T(2,128)} %bitcast.2, f32[1,4,2,32]{3,2,1,0:T(2,128)} %bitcast.3, s32[4,1,32]{2,1,0:T(1,128)} %examples.1, bf16[4,32,3072]{2,1,0:T(8,128)(2,1)} %top.1, bf16[1,4,32,3072]{3,2,1,0:T(8,128)(2,1)} %branch.1, bf16[1,1,4,32,8192]{4,3,2,1,0:T(8,128)(2,1)} %hidden.1, ...), custom_call_target="tpu_custom_call" | custom-call | flops 1342177280 | bytes 16777216 | tf_op jit(solution)/shard_map/pallas_call | solution.py:496
  39.1 1.9 %broadcast_multiply_fusion = f32[1,1,256,512]{3,2,1,0:T(8,128)} fusion(f32[1,1,256,512]{3,2,1,0:T(8,128)} %shard_map.82), kind=kLoop, calls=%fused_computation | loop fusion | flops 131072 | bytes 1048576 | tf_op jit(solution)/shard_map/div | solution.py:549

commit v7 on v6

--- a/solution.py
+++ b/solution.py
@@ -8,11 +8,11 @@
 from jax.sharding import PartitionSpec as P
 
 SEQS = 2
-CHUNK = 128
-IN_FLIGHT = 4
-SWAP_LAG = 3
+CHUNK = 256
+IN_FLIGHT = 3
+SWAP_LAG = 2
 ROWS_LAG = 2
-HOP_LAG = 3
+HOP_LAG = 2
 MESH = pl.DeviceIdType.MESH
 
 
@@ -274,7 +274,7 @@
     def dispatch(c):
         swap_copy(c).wait_recv()
         select = select_v[...]
-        slot_prob = prob_v[:, :1]
+        slot_prob = jnp.concatenate([prob_v[...]] * (chunk // prob_v.shape[1]), axis=1)
 
         def picked(cotangent):
             wide = cotangent.reshape(flat, chunk)
@@ -299,31 +299,35 @@
         rows_all[core, c, low] = mine[:rows]
         rows_all[core, c, 1 - low] = rest[:rows]
 
-    def rotate_model(c):
-        rows_copy(c).wait_recv()
+    batch = 2 if chunks % 2 == 0 else 1
+
+    def rotate_model(index):
+        each = [(index * batch + part, h) for part in range(batch) for h in range(2)]
+        for part in range(batch):
+            rows_copy(index * batch + part).wait_recv()
         total = jnp.dot(
             jnp.concatenate(
                 [
                     jnp.concatenate([rows_all[0, c, h], rows_all[1, c, h]], axis=0)
-                    for h in range(2)
+                    for c, h in each
                 ],
                 axis=1,
             ),
             jnp.concatenate(
                 [
                     bm_v[pl.ds(pl.multiple_of(h * half + c * chunk, 128), chunk), :]
-                    for h in range(2)
+                    for c, h in each
                 ],
                 axis=0,
             ),
             preferred_element_type=jnp.float32,
         )
 
-        @pl.when(c == 0)
+        @pl.when(index == 0)
         def _():
             model_sum[...] = total
 
-        @pl.when(c > 0)
+        @pl.when(index > 0)
         def _():
             model_sum[...] += total
 
@@ -376,7 +380,7 @@
     early = high < last - 1
     held = jnp.minimum(chunks - 1, HOP_LAG * high)
     lag = jnp.where(high > 0, jnp.maximum(chunks, held + SWAP_LAG), held + SWAP_LAG)
-    model_lag = lag + ROWS_LAG
+    model_lag = lag + ROWS_LAG - 1
 
     @pl.when(early)
     def _():
@@ -428,9 +432,11 @@
         def _():
             dispatch(k - lag)
 
-        @pl.when(k >= model_lag)
-        def _():
-            rotate_model(k - model_lag)
+        ready = k - model_lag
+
+        @pl.when(jnp.logical_and(ready >= 0, lax.rem(ready + batch, batch) == batch - 1))
+        def _():
+            rotate_model(ready // batch)
 
         return 0
 

time: 41.1 us -> 41.1 us (level)
  no operation moved by 1% of the time
where the time goes in v7:
time: 41.1 us; the launch traced here: 40.9 us
  Pallas kernels  39 us (95%)
  other arithmetic  1.88 us (5%)
    pallas_call x1, Pallas kernels, on_device(): pl.pallas_call(functools.partial(kernel, sections), out_shape=jax.ShapeDt...  39 us
    div x1, other arithmetic, on_device(): return square_sum / (batches * lax.axis_size('expert') * SEQS)  1.88 us

profile of v7, /device:TPU:0, one launch (start us, length us, event | category | flops | bytes accessed | tf_op | source)
XLA Modules:
  0.0 40.9 jit_solution(4276652479417945341)
XLA Ops:
  0.0 39.0 %shard_map.82 = f32[1,1,256,512]{3,2,1,0:T(8,128)} custom-call(s32[1,4,2,32]{3,2,1,0:T(2,128)} %bitcast.2, f32[1,4,2,32]{3,2,1,0:T(2,128)} %bitcast.3, s32[4,1,32]{2,1,0:T(1,128)} %examples.1, bf16[4,32,3072]{2,1,0:T(8,128)(2,1)} %top.1, bf16[1,4,32,3072]{3,2,1,0:T(8,128)(2,1)} %branch.1, bf16[1,1,4,32,8192]{4,3,2,1,0:T(8,128)(2,1)} %hidden.1, ...), custom_call_target="tpu_custom_call" | custom-call | flops 1342177280 | bytes 16777216 | tf_op jit(solution)/shard_map/pallas_call | solution.py:502
  39.1 1.9 %broadcast_multiply_fusion = f32[1,1,256,512]{3,2,1,0:T(8,128)} fusion(f32[1,1,256,512]{3,2,1,0:T(8,128)} %shard_map.82), kind=kLoop, calls=%fused_computation | loop fusion | flops 131072 | bytes 1048576 | tf_op jit(solution)/shard_map/div | solution.py:555

commit v8 on v7

--- a/solution.py
+++ b/solution.py
@@ -396,6 +396,8 @@
         def _():
             rotate_hidden()
 
+        prepare_hidden()
+
     def step(k, _):
         @pl.when(k < chunks)
         def _():
@@ -419,7 +421,7 @@
             def _():
                 rotate_hidden()
 
-        @pl.when(k == jnp.where(high > 0, chunks + 1, chunks // 2))
+        @pl.when(jnp.logical_and(k == chunks + 1, high > 0))
         def _():
             prepare_hidden()
 

time: 41.1 us -> 41.1 us (level)
  no operation moved by 1% of the time
where the time goes in v8:
time: 41.1 us; the launch traced here: 40.9 us
  Pallas kernels  39 us (95%)
  other arithmetic  1.88 us (5%)
    pallas_call x1, Pallas kernels, on_device(): pl.pallas_call(functools.partial(kernel, sections), out_shape=jax.ShapeDt...  39 us
    div x1, other arithmetic, on_device(): return square_sum / (batches * lax.axis_size('expert') * SEQS)  1.88 us

profile of v8, /device:TPU:0, one launch (start us, length us, event | category | flops | bytes accessed | tf_op | source)
XLA Modules:
  0.0 40.9 jit_solution(10528555825009868125)
XLA Ops:
  0.0 39.0 %shard_map.82 = f32[1,1,256,512]{3,2,1,0:T(8,128)} custom-call(s32[1,4,2,32]{3,2,1,0:T(2,128)} %bitcast.2, f32[1,4,2,32]{3,2,1,0:T(2,128)} %bitcast.3, s32[4,1,32]{2,1,0:T(1,128)} %examples.1, bf16[4,32,3072]{2,1,0:T(8,128)(2,1)} %top.1, bf16[1,4,32,3072]{3,2,1,0:T(8,128)(2,1)} %branch.1, bf16[1,1,4,32,8192]{4,3,2,1,0:T(8,128)(2,1)} %hidden.1, ...), custom_call_target="tpu_custom_call" | custom-call | flops 1342177280 | bytes 16777216 | tf_op jit(solution)/shard_map/pallas_call | solution.py:504
  39.1 1.9 %broadcast_multiply_fusion = f32[1,1,256,512]{3,2,1,0:T(8,128)} fusion(f32[1,1,256,512]{3,2,1,0:T(8,128)} %shard_map.82), kind=kLoop, calls=%fused_computation | loop fusion | flops 131072 | bytes 1048576 | tf_op jit(solution)/shard_map/div | solution.py:557
